TPU v7x, 32 devices: a whole 2x2x4 slice. The times are simulated.
32 devices in a mesh: layer: 4 (over y, x), row: 8 (over z, core).
Axes of the slice: x: 2, y: 2, z: 4, core: 2. Of those that a mesh axis runs over, the one named last changes fastest.
Arguments:
- tokens: bfloat16 [16, 8192], P('row'), may hold values from -6 to 6
- up_weight: bfloat16 [4, 32768, 8192], P('layer', 'row'), may hold values from -6 to 6
- hess_panel: float32 [4, 256, 8192], P('layer', None, 'row'), may hold values from -1 to 2, as said below
- keep_mask: int32 [4, 32768, 256], P('layer', 'row'), may hold values from 0 to 1, as said below
Outputs:
- section_acts: bfloat16 [4, 16, 8192], P('layer', 'row')
- pruned_blocks: bfloat16 [4, 32768, 256], P('layer', 'row')
Inputs may be any that keep to these rules, and one draw needn't show every extreme that they name: `keep_mask`: each row has exactly 64 ones in each block of 128 columns. `hess_panel`: zero where the column is below the row; the diagonal lies in [0.5, 2].
All inputs are finite; a program needn't handle non-finite values.
Results may differ from a plain program's by a relative error of at most 0.017.
Values may be sent and summed in bfloat16 or wider, within the bound.
No kernel may reach another device: no remote copies, remote signals or barrier semaphores. Data moves between devices by JAX's collectives and lax.ppermute only.
A program may use at most 384 MiB of HBM per device.

v0:
```python
import functools

import jax
import jax.numpy as jnp
from jax import lax
from jax.experimental import pallas as pl
from jax.experimental.pallas import tpu as pltpu
from jax.sharding import PartitionSpec as P

BLOCK = 128
SUB = 16
ELIMINATE_VMEM = 46 * 1024 * 1024
TURN_VMEM = 36 * 1024 * 1024

epsilon = 1e-05


def gathered(array, axis):
    size = lax.axis_size(axis)
    copies = jnp.broadcast_to(array[None], (size,) + array.shape)
    return lax.all_to_all(copies, axis, split_axis=0, concat_axis=0)


def nt_dot(left, right):
    return lax.dot_general(
        left, right, (((1,), (1,)), ((), ())), preferred_element_type=jnp.float32
    )


def nn_dot(left, right):
    return jnp.dot(left, right, preferred_element_type=jnp.float32)


def split_halves(value):
    high = value.astype(jnp.bfloat16)
    low = (value - high.astype(jnp.float32)).astype(jnp.bfloat16)
    return high, low


def identity(count):
    row = lax.broadcasted_iota(jnp.int32, (count, count), 0)
    column = lax.broadcasted_iota(jnp.int32, (count, count), 1)
    return jnp.where(row == column, 1.0, 0.0).astype(jnp.bfloat16)


def eliminate_kernel(scale, part_rows, where_ref, scalar_ref, inverse_ref, inner_ref, cross_ref, weight_ref,
                     mask_ref, product_ref, inputs_ref, panel_ref, whole_ref, pruned_ref, aux_ref, out_ref,
                     state, dropped, errors, ring, own_product, sems):
    count = 2 * BLOCK
    depth = count * 8
    sheets = state.shape[0] // depth
    lanes = sheets * 128
    spots = [(g, q, slice((g * sheets + q) * 128, (g * sheets + q + 1) * 128))
             for g in range(8) for q in range(sheets)]

    def place(g, q, first, size):
        return pl.ds(q * depth + first * 8 + g, size, stride=8)

    def plane(q, j):
        return slice(q * depth + j * 8, q * depth + (j + 1) * 8)

    tile_index = pl.program_id(0)
    slots, chunk, _ = ring.shape

    def fetch(tile, slot):
        row = pl.multiple_of(tile * part_rows + part_rows // 2 + slot * chunk, chunk)
        return chunk_copy(whole_ref, ring.at[slot], sems.at[slot], row)

    @pl.when(tile_index == 0)
    def _():
        for slot in range(slots):
            fetch(0, slot).start()

    def multiply(slot):
        fetch(tile_index, slot).wait()
        own_product[:, slot * chunk : (slot + 1) * chunk] = nt_dot(inputs_ref[:, count:], ring[slot])

    def renew(slot):
        @pl.when(tile_index + 1 < pl.num_programs(0))
        def _():
            fetch(tile_index + 1, slot).start()

    eye = identity(count)
    columns = nt_dot(eye, weight_ref[...])
    drops = nt_dot(eye, (1 - mask_ref[...]).astype(jnp.float32).astype(jnp.bfloat16))
    for g, q, where in spots:
        state[place(g, q, 0, count), :] = columns[:, where]
        dropped[place(g, q, 0, count), :] = drops[:, where]

    def stacked(first, size):
        wide = jnp.concatenate([errors[place(g, q, first, size), :] for g, q, _ in spots], 1)
        return jnp.concatenate(split_halves(wide), 0)

    def subtract(product, first, size):
        for g, q, where in spots:
            at = place(g, q, first, size)
            state[at, :] = state[at, :] - product[:, where]

    for block in range(2):
        for part in range(BLOCK // SUB):
            first = block * BLOCK + part * SUB
            spread = 2 * (BLOCK // SUB) // slots
            slot, at_slot = divmod(block * (BLOCK // SUB) + part, spread)
            if at_slot == spread // 2:
                multiply(slot)
            planes = [[state[plane(q, first + i), :] for q in range(sheets)] for i in range(SUB)]
            for i in range(SUB):
                j = first + i
                inverse = inverse_ref[j]
                error = []
                for q in range(sheets):
                    lost = planes[i][q] * dropped[plane(q, j), :]
                    error.append(lost * inverse)
                    state[plane(q, j), :] = planes[i][q] - lost
                    errors[plane(q, j), :] = error[q]
                for k in range(i + 1, SUB):
                    scalar = scalar_ref[j * SUB + k]
                    for q in range(sheets):
                        planes[k][q] = planes[k][q] - error[q] * scalar
            after = first + SUB
            left = (block + 1) * BLOCK - after
            if left:
                factor = inner_ref[block * (BLOCK // SUB) + part, after : after + left, :]
                subtract(nn_dot(factor, stacked(first, SUB)), after, left)
            if at_slot == spread - 1:
                renew(slot)
        if block == 0:
            subtract(nn_dot(cross_ref[...], stacked(0, BLOCK)), BLOCK, BLOCK)

    small = identity(128)
    for g, q, where in spots:
        kept = state[place(g, q, 0, count), :].astype(jnp.bfloat16)
        aux_ref[0:count, where] = kept
        aux_ref[count:, where] = errors[place(g, q, 0, count), :].astype(jnp.bfloat16)
        pruned_ref[where, :] = nt_dot(small, kept).astype(jnp.bfloat16)

    half = part_rows // 2
    step = min(512, half)
    for first in range(0, part_rows, step):
        place = slice(first, first + step)
        change = corrected(inputs_ref[:, :count], panel_ref[...], aux_ref, place)
        source, at = (product_ref, first) if first < half else (own_product, first - half)
        value = source[:, at : at + step] + change
        base = tile_index * part_rows + first
        out_ref[:, place] = units_of(value, inputs_ref, where_ref, base, scale)


def tile_rows(given):
    return 2048 if given % 2048 == 0 else 1024


def eliminate(weight, factor, mask, where, product, inputs, panel_inputs, scale):
    count = 2 * BLOCK
    given = weight.shape[0]
    whole = weight
    rows = pl.cdiv(given, 1024) * 1024
    if rows != given:
        more = ((0, rows - given), (0, 0))
        weight, mask = jnp.pad(weight[:, :count], more), jnp.pad(mask, more)
    tile = tile_rows(given)
    subs = count // SUB
    wide = factor.astype(jnp.float32)
    row = lax.broadcasted_iota(jnp.int32, wide.shape, 0)
    column = lax.broadcasted_iota(jnp.int32, wide.shape, 1)
    inverse = 1.0 / jnp.sum(jnp.where(row == column, wide, 0.0), axis=1)
    near = jnp.where(row // SUB == column // SUB, wide, 0.0)
    scalars = near.reshape(count, subs, SUB).sum(axis=1).reshape(-1)
    columns = factor.T.reshape(count, subs, SUB).transpose(1, 0, 2)
    inner = jnp.concatenate([columns, columns], 2)
    cross = factor[:BLOCK, BLOCK:].T
    cross = jnp.concatenate([cross, cross], 1)
    smem = pl.BlockSpec(memory_space=pltpu.SMEM)
    tokens = inputs.shape[0]
    part = min(given, tile)
    chunk = min(256, part // 2)
    slots = part // 2 // chunk
    hbm = pltpu.MemorySpace.HBM
    pruned, aux, units = pl.pallas_call(
        functools.partial(eliminate_kernel, scale, part),
        grid=(rows // tile,),
        in_specs=[
            smem,
            smem,
            smem,
            pl.BlockSpec((subs, count, 2 * SUB), lambda i: (0, 0, 0)),
            pl.BlockSpec((BLOCK, count), lambda i: (0, 0)),
            pl.BlockSpec((tile, count), lambda i: (i, 0)),
            pl.BlockSpec((tile, count), lambda i: (i, 0)),
            pl.BlockSpec((tokens, part // 2), lambda i: (0, i)),
            pl.BlockSpec(inputs.shape, lambda i: (0, 0)),
            pl.BlockSpec((tokens, count), lambda i: (0, 0)),
            pl.BlockSpec(memory_space=hbm),
        ],
        out_specs=[
            pl.BlockSpec((tile, count), lambda i: (i, 0)),
            pl.BlockSpec((2 * count, tile), lambda i: (0, i)),
            pl.BlockSpec((tokens, part), lambda i: (0, i)),
        ],
        out_shape=[
            jax.ShapeDtypeStruct((rows, count), jnp.bfloat16),
            hbm((2 * count, rows), jnp.bfloat16),
            jax.ShapeDtypeStruct((tokens, given), jnp.bfloat16),
        ],
        scratch_shapes=[pltpu.VMEM((tile * count // 128, 128), jnp.float32)] * 3 + [
            pltpu.VMEM((slots, chunk, inputs.shape[1] - count), jnp.bfloat16),
            pltpu.VMEM((tokens, part // 2), jnp.float32),
            pltpu.SemaphoreType.DMA((slots,)),
        ],
        compiler_params=pltpu.CompilerParams(vmem_limit_bytes=ELIMINATE_VMEM),
        cost_estimate=pl.CostEstimate(
            flops=2 * rows * count * count, bytes_accessed=rows * count * 12, transcendentals=0
        ),
        name="eliminate",
    )(
        where, scalars, inverse, inner, cross, weight,
        pltpu.with_memory_space_constraint(mask, hbm), product, inputs, panel_inputs, whole,
    )
    return pruned[:given], aux[:, :given], units


def corrected(lead, panel_inputs, aux_ref, place):
    count = 2 * BLOCK
    tokens = lead.shape[0]
    both = nn_dot(jnp.concatenate(split_halves(panel_inputs), 0), aux_ref[count:, place])
    return nn_dot(lead, aux_ref[0:count, place]) - both[:tokens] - both[tokens:]


def units_of(value, inputs, where_ref, first, scale):
    units = (value * scale).astype(jnp.bfloat16).astype(jnp.float32)
    units = units / (1.0 + jnp.exp(-units))
    at = pl.ds(pl.multiple_of(where_ref[0] + first, 128), value.shape[1])
    units = units + inputs[:, at].astype(jnp.float32) * where_ref[1].astype(jnp.float32)
    return units.astype(jnp.bfloat16)


def fold_kernel(spread_ref, copies_ref, produced_ref):
    peers, own, features = copies_ref.shape
    rows = spread_ref.shape[2]
    parts = []
    for first in range(0, features, rows):
        part = None
        for peer in range(peers):
            if peer * rows % features == first:
                units = spread_ref[peer].astype(jnp.float32)
                part = units if part is None else part + units
        parts.append(part)
    combined = jnp.concatenate(parts, 1)
    moment = jnp.sum(combined * combined, axis=1, keepdims=True) * (1.0 / features)
    produced = (combined * lax.rsqrt(moment + epsilon)).astype(jnp.bfloat16)
    produced_ref[...] = produced
    for peer in range(peers):
        copies_ref[peer] = produced


def fold(spread, peers, features):
    own = spread.shape[1]
    return pl.pallas_call(
        fold_kernel,
        in_specs=[pl.BlockSpec(memory_space=pltpu.VMEM)],
        out_specs=[pl.BlockSpec(memory_space=pltpu.VMEM)] * 2,
        out_shape=[
            jax.ShapeDtypeStruct((peers, own, features), jnp.bfloat16),
            jax.ShapeDtypeStruct((own, features), jnp.bfloat16),
        ],
        compiler_params=pltpu.CompilerParams(vmem_limit_bytes=8 * 1024 * 1024),
        name="fold",
    )(spread)


def chunk_copy(weight_ref, target, sem, row):
    chunk, width = target.shape
    skipped = weight_ref.shape[1] - width
    return pltpu.make_async_copy(
        weight_ref.at[pl.ds(row, chunk), pl.ds(skipped, width)], target, sem
    )


def stream(weight_ref, ring, ring_sems, total, row_of, inputs, use):
    slots = ring.shape[0]

    def copy(index, slot):
        return chunk_copy(weight_ref, ring.at[slot], ring_sems.at[slot], row_of(index))

    def begin():
        for index in range(slots):
            copy(index, index).start()

    def step(index, _):
        slot = lax.rem(index, slots)
        copy(index, slot).wait()
        use(index, nt_dot(inputs(), ring[slot]))

        @pl.when(index + slots < total)
        def _():
            copy(index + slots, slot).start()

        return 0

    def run():
        lax.fori_loop(0, total, step, 0)

    return begin, run


def first_kernel(part_rows, inputs_ref, weight_ref, product_ref, ring, ring_sems):
    chunk, width = ring.shape[1:]
    skipped = weight_ref.shape[1] - width
    each = part_rows // 2 // chunk

    def row_of(index):
        return pl.multiple_of(index // each * part_rows + index % each * chunk, chunk)

    def use(index, product):
        product_ref[:, pl.ds(pl.multiple_of(index * chunk, chunk), chunk)] = product

    total = product_ref.shape[1] // chunk
    begin, run = stream(
        weight_ref, ring, ring_sems, total, row_of, lambda: inputs_ref[:, skipped:], use
    )
    begin()
    run()


def first_product(inputs, weight):
    tokens, features = inputs.shape
    rows = weight.shape[0]
    width = features - 2 * BLOCK
    part = min(rows, tile_rows(rows))
    chunk = min(256, part // 2)
    ring = (min(6, rows // 2 // chunk), chunk, width)
    return pl.pallas_call(
        functools.partial(first_kernel, part),
        in_specs=[
            pl.BlockSpec(memory_space=pltpu.VMEM),
            pl.BlockSpec(memory_space=pltpu.MemorySpace.HBM),
        ],
        out_specs=pl.BlockSpec(memory_space=pltpu.VMEM),
        out_shape=jax.ShapeDtypeStruct((tokens, rows // 2), jnp.float32),
        scratch_shapes=[pltpu.VMEM(ring, jnp.bfloat16), pltpu.SemaphoreType.DMA((ring[0],))],
        compiler_params=pltpu.CompilerParams(vmem_limit_bytes=32 * 1024 * 1024),
        cost_estimate=pl.CostEstimate(
            flops=tokens * rows * width, bytes_accessed=rows * width, transcendentals=0
        ),
        name="first_product",
    )(inputs, weight)


def turn_kernel(scale, where_ref, inputs_ref, weight_ref, panel_ref, aux_ref, out_ref, ring, panel,
                aux, change, ring_sems, side_sems):
    chunk, width = ring.shape[1:]
    skipped = weight_ref.shape[1] - width

    def place_of(index):
        return pl.multiple_of(index * chunk, chunk)

    def use(index, product):
        place = pl.ds(place_of(index), chunk)
        value = product + change[:, place]
        out_ref[:, place] = units_of(value, inputs_ref, where_ref, place_of(index), scale)

    rows = change.shape[1]
    begin, run = stream(
        weight_ref, ring, ring_sems, rows // chunk, place_of, lambda: inputs_ref[:, skipped:], use
    )
    panel_copy = pltpu.make_async_copy(
        panel_ref.at[:, pl.ds(skipped, width)], panel, side_sems.at[0]
    )
    aux_copy = pltpu.make_async_copy(aux_ref, aux, side_sems.at[1])
    panel_copy.start()
    aux_copy.start()
    begin()
    panel_copy.wait()
    panel_inputs = nt_dot(inputs_ref[:, skipped:], panel[...])
    aux_copy.wait()
    step = min(1024, rows)
    for first in range(0, rows, step):
        place = slice(first, first + step)
        change[:, place] = corrected(inputs_ref[:, :skipped], panel_inputs, aux, place)
    run()


def turn_product(where, inputs, weight, panel, aux, scale):
    tokens, features = inputs.shape
    rows = weight.shape[0]
    count = 2 * BLOCK
    width = features - count
    chunk = min(256, rows // 2)
    ring = (min(6, rows // chunk), chunk, width)
    vmem = pl.BlockSpec(memory_space=pltpu.VMEM)
    hbm = pl.BlockSpec(memory_space=pltpu.MemorySpace.HBM)
    return pl.pallas_call(
        functools.partial(turn_kernel, scale),
        in_specs=[pl.BlockSpec(memory_space=pltpu.SMEM), vmem, hbm, hbm, hbm],
        out_specs=vmem,
        out_shape=jax.ShapeDtypeStruct((tokens, rows), jnp.bfloat16),
        scratch_shapes=[
            pltpu.VMEM(ring, jnp.bfloat16),
            pltpu.VMEM((count, width), jnp.bfloat16),
            pltpu.VMEM(aux.shape, jnp.bfloat16),
            pltpu.VMEM((tokens, rows), jnp.float32),
            pltpu.SemaphoreType.DMA((ring[0],)),
            pltpu.SemaphoreType.DMA((2,)),
        ],
        compiler_params=pltpu.CompilerParams(vmem_limit_bytes=TURN_VMEM),
        cost_estimate=pl.CostEstimate(
            flops=2 * tokens * rows * features, bytes_accessed=rows * width * 2, transcendentals=0
        ),
        name="turn_product",
    )(where, inputs, weight, panel, aux)


def per_device(tokens, up_weight, hess_panel, keep_mask):
    weight = up_weight[0]
    local_panel = hess_panel[0].astype(jnp.bfloat16)
    count = 2 * BLOCK
    features = weight.shape[1]
    scale = features ** (-0.5)
    row_size = lax.axis_size("row")
    own = tokens.shape[0]
    held = local_panel.shape[1]
    position = lax.axis_index("layer")
    depth = lax.axis_size("layer")
    start = lax.axis_index("row") * held

    width = min(count, held)
    share = count // row_size
    factor_share = local_panel[:, :width].reshape(row_size, share * width // count, count)
    cut = own * features // count
    token_share = jnp.broadcast_to(tokens.reshape(1, cut, count), (row_size, cut, count))
    first = lax.all_to_all(
        jnp.concatenate([token_share, factor_share], 1), "row", split_axis=0, concat_axis=0
    )
    first, local_panel = lax.optimization_barrier((first, local_panel))
    portion = first[:, :cut].reshape(row_size * own, features)
    full_panel = lax.all_gather(local_panel, "row", axis=1, tiled=True)

    owned = [first[o, cut:].reshape(share, width) for o in range(count // width)]
    column = lax.broadcasted_iota(jnp.int32, local_panel.shape, 1) + start
    remote = jnp.where(column < count, jnp.zeros_like(local_panel), local_panel)
    partial_sum = nt_dot(lax.dynamic_slice_in_dim(portion, start, held, 1), remote)
    shares = jnp.concatenate([jnp.concatenate(owned, 1), *split_halves(partial_sum)], 0)
    shares, portion = lax.optimization_barrier((shares, portion))
    second = gathered(shares, "row")
    factor = second[:, :share].reshape(count, count)
    sums = second[:, share:].astype(jnp.float32).reshape(row_size, 2, row_size * own, count)

    product = first_product(portion, weight)
    rows = weight.shape[0]
    from_row = lax.axis_index("row") * rows
    where = jnp.stack([from_row % features, (from_row < features).astype(jnp.int32)])
    pruned, aux, units = eliminate(
        weight, factor, keep_mask[0], where, product, portion, sums.sum(axis=(0, 1)), scale
    )
    results = jnp.zeros_like(tokens)
    for turn in range(depth):
        last = turn + 1 == depth
        if turn:
            portion = copies.reshape(row_size * own, features)
            units = turn_product(where, portion, weight, full_panel, aux, scale)
        units = units.reshape(row_size, own, rows)
        if last:
            spread = lax.all_to_all(units, "row", split_axis=0, concat_axis=0)
        else:
            pair = [turn, turn + 1]
            others = [layer for layer in range(depth) if layer not in pair]
            groups = [
                [layer * row_size + peer for layer in layers for peer in range(row_size)]
                for layers in [pair] + [others[i : i + 2] for i in range(0, len(others), 2)]
            ]
            spread = lax.all_to_all(
                jnp.concatenate([units, units], 0), ("layer", "row"), split_axis=0, concat_axis=0, axis_index_groups=groups
            )
        copies, produced = fold(spread, row_size, features)
        results = jnp.where(position == turn, produced, results)
        if not last:
            copies = lax.all_to_all(copies, "row", split_axis=0, concat_axis=0)
    return (results[None], pruned[None])


def solution(mesh):
    in_specs = (
        P("row", None),
        P("layer", "row", None),
        P("layer", None, "row"),
        P("layer", "row", None),
    )
    out_specs = (P("layer", "row", None), P("layer", "row", None))
    return jax.shard_map(
        per_device, mesh=mesh, in_specs=in_specs, out_specs=out_specs, check_vma=False
    )
```

profile of v0, /device:TPU:0, one launch (start us, length us, event | category | flops | bytes accessed | tf_op | source)
XLA Modules:
  0.0 267.7 jit_solution(9473051095036276441)
XLA Ops:
  7.2 1.3 convert_bitcast_fusion
  8.5 0.8 broadcast_in_dim.32
  9.4 18.7 %all_to_all.45 = bf16[8,96,256]{2,1,0:T(8,128)(2,1)S(1)} all-to-all(bf16[8,96,256]{2,1,0:T(8,128)(2,1)S(1)} %pad_maximum_fusion), channel_id=1, replica_groups=mesh['layer'=4,'row'=8] {'row'}, dimensions={0} | all-to-all | bytes 786432 | tf_op jit(solution)/shard_map/all_to_all | solution.py:430
  28.2 0.1 reshape.102.inputs_ref
  28.4 1.3 subtract_convert_fusion
  29.7 0.7 broadcast_in_dim.35
  30.4 3.4 %all-to-all-start.1 = ((bf16[8,64,256]{2,1,0:T(8,128)(2,1)}), bf16[8,64,256]{2,1,0:T(8,128)(2,1)S(1)}, u32[]{:S(2)}, u32[]{:S(2)}) async-start(bf16[8,64,256]{2,1,0:T(8,128)(2,1)} %broadcast_in_dim.35), calls=%async_computation.1 | async-start | bytes 524288 | tf_op jit(solution)/shard_map/all_to_all | solution.py:21
  33.9 12.4 %first_product.1.product_ref = f32[16,2048]{1,0:T(8,128)S(1)} custom-call(bf16[16,8192]{1,0:T(8,128)(2,1)S(1)} %reshape.102.inputs_ref, bf16[4096,8192]{1,0:T(8,128)(2,1)} %bitcast.10.weight_ref.whole_ref), custom_call_target="tpu_custom_call" | custom-call | flops 520093696 | bytes 32505856 | tf_op jit(solution)/shard_map/first_product/pallas_call | solution.py:331
  46.3 2.3 all-to-all-done.1
  48.7 0.4 copy.15
  49.1 0.3 reshape.114
  49.4 0.2 select_reduce_fusion.1
  49.6 0.1 copy.16
  49.7 0.1 reshape.103.scalar_ref
  49.8 0.5 copy.18.inner_ref
  50.3 0.1 copy.19
  50.4 0.2 convert_reduce_fusion
  50.7 31.5 %eliminate.1 = (bf16[4096,256]{1,0:T(8,128)(2,1)}, bf16[512,4096]{1,0:T(8,128)(2,1)}, bf16[16,4096]{1,0:T(8,128)(2,1)S(1)}) custom-call(s32[2]{0:T(128)S(1)} %pad_add_fusion.where_ref, f32[4096]{0:T(1024)S(1)} %reshape.103.scalar_ref, f32[256]{0:T(256)S(1)} %div.30.inverse_ref, bf16[16,256,32]{2,1,0:T(8,128)(2,1)S(1)} %copy.18.inner_ref, ...), custom_call_target="tpu_custom_call" | custom-call | flops 536870912 | bytes 12582912 | tf_op jit(solution)/shard_map/eliminate/pallas_call | solution.py:178
  82.2 0.1 reshape.106
  82.4 0.3 pad_maximum_fusion.2
  82.7 15.3 %all_to_all.46.spread_ref = bf16[16,2,4096]{2,1,0:T(2,128)(2,1)S(1)} all-to-all(bf16[16,2,4096]{2,1,0:T(2,128)(2,1)S(1)} %pad_maximum_fusion.2), channel_id=1, replica_groups={{0,1,2,3,4,5,6,7,8,9,10,11,12,13,14,15},{16,17,18,19,20,21,22,23,24,25,..., dimensions={0} | all-to-all | bytes 524288 | tf_op jit(solution)/shard_map/all_to_all | solution.py:470
  98.0 0.2 fold.4
  98.2 12.2 %all_to_all.47 = bf16[8,2,8192]{2,1,0:T(2,128)(2,1)S(1)} all-to-all(bf16[8,2,8192]{2,1,0:T(2,128)(2,1)S(1)} %get-tuple-element.21), channel_id=1, replica_groups=mesh['layer'=4,'row'=8] {'row'}, dimensions={0} | all-to-all | bytes 524288 | tf_op jit(solution)/shard_map/all_to_all | solution.py:476
  110.4 0.1 reshape.107.inputs_ref
  110.6 2.2 copy-done
  112.8 2.2 copy-done.3
  115.0 23.6 %turn_product.3 = bf16[16,4096]{1,0:T(8,128)(2,1)S(1)} custom-call(s32[2]{0:T(128)S(1)} %pad_add_fusion.where_ref, bf16[16,8192]{1,0:T(8,128)(2,1)S(1)} %reshape.107.inputs_ref, bf16[4096,8192]{1,0:T(8,128)(2,1)} %bitcast.10.weight_ref.whole_ref, bf16[256,8192]{1,0:T(8,128)(2,1)S(1)} %copy-done, bf16[512,4096]{1,0:T(8,128)(2,1)S(1)} %copy-done.3), custom_call_target="tpu_custom_call" | custom-call | flops 1073741824 | bytes 65011712 | tf_op jit(solution)/shard_map/turn_product/pallas_call | solution.py:391
  138.6 0.1 reshape.108
  138.7 0.3 pad_maximum_fusion.3
  139.1 14.2 %all_to_all.48.spread_ref = bf16[16,2,4096]{2,1,0:T(2,128)(2,1)S(1)} all-to-all(bf16[16,2,4096]{2,1,0:T(2,128)(2,1)S(1)} %pad_maximum_fusion.3), channel_id=1, replica_groups={{8,9,10,11,12,13,14,15,16,17,18,19,20,21,22,23},{0,1,2,3,4,5,6,7,24,25,..., dimensions={0} | all-to-all | bytes 524288 | tf_op jit(solution)/shard_map/all_to_all | solution.py:470
  153.3 0.2 fold.5
  153.5 12.2 %all_to_all.49 = bf16[8,2,8192]{2,1,0:T(2,128)(2,1)S(1)} all-to-all(bf16[8,2,8192]{2,1,0:T(2,128)(2,1)S(1)} %get-tuple-element.23), channel_id=1, replica_groups=mesh['layer'=4,'row'=8] {'row'}, dimensions={0} | all-to-all | bytes 524288 | tf_op jit(solution)/shard_map/all_to_all | solution.py:476
  165.9 2.2 copy-done.1
  168.1 2.2 copy-done.4
  170.2 23.6 %turn_product.4 = bf16[16,4096]{1,0:T(8,128)(2,1)S(1)} custom-call(s32[2]{0:T(128)S(1)} %pad_add_fusion.where_ref, bf16[16,8192]{1,0:T(8,128)(2,1)S(1)} %reshape.109.inputs_ref, bf16[4096,8192]{1,0:T(8,128)(2,1)} %bitcast.10.weight_ref.whole_ref, bf16[256,8192]{1,0:T(8,128)(2,1)S(1)} %copy-done.1, bf16[512,4096]{1,0:T(8,128)(2,1)S(1)} %copy-done.4), custom_call_target="tpu_custom_call" | custom-call | flops 1073741824 | bytes 65011712 | tf_op jit(solution)/shard_map/turn_product/pallas_call | solution.py:391
  193.9 0.1 reshape.110
  194.0 0.3 pad_maximum_fusion.4
  194.3 13.5 %all_to_all.50.spread_ref = bf16[16,2,4096]{2,1,0:T(2,128)(2,1)S(1)} all-to-all(bf16[16,2,4096]{2,1,0:T(2,128)(2,1)S(1)} %pad_maximum_fusion.4), channel_id=1, replica_groups={{16,17,18,19,20,21,22,23,24,25,26,27,28,29,30,31},{0,1,2,3,4,5,6,7,8,9,..., dimensions={0} | all-to-all | bytes 524288 | tf_op jit(solution)/shard_map/all_to_all | solution.py:470
  207.8 0.2 fold.6
  208.1 12.2 %all_to_all.51 = bf16[8,2,8192]{2,1,0:T(2,128)(2,1)S(1)} all-to-all(bf16[8,2,8192]{2,1,0:T(2,128)(2,1)S(1)} %get-tuple-element.24), channel_id=1, replica_groups=mesh['layer'=4,'row'=8] {'row'}, dimensions={0} | all-to-all | bytes 524288 | tf_op jit(solution)/shard_map/all_to_all | solution.py:476
  220.4 2.2 copy-done.2
  222.6 2.2 copy-done.5
  224.8 23.6 %turn_product.5 = bf16[16,4096]{1,0:T(8,128)(2,1)S(1)} custom-call(s32[2]{0:T(128)S(1)} %pad_add_fusion.where_ref, bf16[16,8192]{1,0:T(8,128)(2,1)S(1)} %reshape.111.inputs_ref, bf16[4096,8192]{1,0:T(8,128)(2,1)} %bitcast.10.weight_ref.whole_ref, bf16[256,8192]{1,0:T(8,128)(2,1)S(1)} %copy-done.2, bf16[512,4096]{1,0:T(8,128)(2,1)S(1)} %copy-done.5), custom_call_target="tpu_custom_call" | custom-call | flops 1073741824 | bytes 65011712 | tf_op jit(solution)/shard_map/turn_product/pallas_call | solution.py:391
  248.4 0.8 reshape.112
  249.2 3.4 %all-to-all-start.8 = ((bf16[8,2,4096]{2,1,0:T(2,128)(2,1)}), bf16[8,2,4096]{2,1,0:T(2,128)(2,1)S(1)}, u32[]{:S(2)}, u32[]{:S(2)}) async-start(bf16[8,2,4096]{2,1,0:T(2,128)(2,1)} %reshape.112), calls=%async_computation.8 | async-start | bytes 262144 | tf_op jit(solution)/shard_map/all_to_all | solution.py:462
  252.6 6.7 %all-to-all-done.8.spread_ref = bf16[8,2,4096]{2,1,0:T(2,128)(2,1)S(1)} async-done(((bf16[8,2,4096]{2,1,0:T(2,128)(2,1)}), bf16[8,2,4096]{2,1,0:T(2,128)(2,1)S(1)}, u32[]{:S(2)}, u32[]{:S(2)}) %all-to-all-start.8) | async-done | bytes 131104 | tf_op jit(solution)/shard_map/all_to_all | solution.py:462
  259.3 0.9 fold.7
  260.2 0.7 fusion.4
  (33 shorter events, 0.6 us)
Async XLA Ops:
  7.2 103.4 %all-gather.2.cloned.1.call-start = ((), (), s32[]{:S(2)}) async-start(), calls=%async_computation.9 | async-start | bytes 4718592 | tf_op jit(solution)/shard_map/all_gather | solution.py:435
  8.5 19.6 %copy-start.6 = (bf16[256,1024]{1,0:T(8,128)(2,1)}, bf16[256,1024]{1,0:T(8,128)(2,1)S(1)}, u32[]{:S(2)}) copy-start(bf16[256,1024]{1,0:T(8,128)(2,1)S(1)} %convert_bitcast_fusion) | copy-start | bytes 1572868
  30.4 18.3 %all-to-all-start.1 = ((bf16[8,64,256]{2,1,0:T(8,128)(2,1)}), bf16[8,64,256]{2,1,0:T(8,128)(2,1)S(1)}, u32[]{:S(2)}, u32[]{:S(2)}) async-start(bf16[8,64,256]{2,1,0:T(8,128)(2,1)} %broadcast_in_dim.35), calls=%async_computation.1 | async-start | bytes 524288 | tf_op jit(solution)/shard_map/all_to_all | solution.py:21
  110.6 2.2 copy-start
  112.8 2.2 copy-start.3
  165.9 2.2 copy-start.1
  168.1 2.2 copy-start.4
  220.4 2.2 copy-start.2
  222.6 2.2 copy-start.5
  249.2 10.1 %all-to-all-start.8 = ((bf16[8,2,4096]{2,1,0:T(2,128)(2,1)}), bf16[8,2,4096]{2,1,0:T(2,128)(2,1)S(1)}, u32[]{:S(2)}, u32[]{:S(2)}) async-start(bf16[8,2,4096]{2,1,0:T(2,128)(2,1)} %reshape.112), calls=%async_computation.8 | async-start | bytes 262144 | tf_op jit(solution)/shard_map/all_to_all | solution.py:462
Sparse Core Ops, SparseCore 0:
  28.2 50.8 all-gather.1
where the time goes:
time: 269 us; the launch traced here: 268 us
  Pallas kernels  116 us (43%)
  blocking collectives  98.4 us (37%)
  local copies, waits for them, and re-layouts  17.8 us (7%)
  between operations  14.4 us (5%)
  waiting for transfers between devices  9.06 us (3%)
  starting transfers between devices  6.82 us (3%)
  other arithmetic  3.58 us (1%)
    pallas_call x3, Pallas kernels, turn_product(): pl.pallas_call(functools.partial(turn_kernel, scale), in_specs=[pl.BlockS...  70.9 us
    all_to_all x3, blocking collectives, per_device(): lax.all_to_all(jnp.concatenate([units, units], 0), ('layer', 'row'), spli...  43 us
    all_to_all x3, blocking collectives, per_device(): copies = lax.all_to_all(copies, 'row', split_axis=0, concat_axis=0)  36.7 us
    pallas_call x1, Pallas kernels, eliminate(): pl.pallas_call(functools.partial(eliminate_kernel, scale, part), grid=(ro...  31.5 us
    all_to_all x1, blocking collectives, per_device(): lax.all_to_all(jnp.concatenate([token_share, factor_share], 1), 'row', sp...  18.7 us
    unnamed x15, local copies, waits for them, and re-layouts  13.2 us
    pallas_call x1, Pallas kernels, first_product(): pl.pallas_call(functools.partial(first_kernel, part), in_specs=[pl.BlockS...  12.4 us
    all_to_all x1, waiting for transfers between devices, per_device(): spread = lax.all_to_all(units, 'row', split_axis=0, concat_axis=0)  6.7 us
  transfers between devices with their start and end apart: 3, of which 2 were waited for; matrix products, arithmetic and copies ran while one was open for 2% of the time, Pallas kernels for 16%

commit v1 on v0

--- a/solution.py
+++ b/solution.py
@@ -9,7 +9,7 @@
 
 BLOCK = 128
 SUB = 16
-ELIMINATE_VMEM = 46 * 1024 * 1024
+ELIMINATE_VMEM = 40 * 1024 * 1024
 TURN_VMEM = 36 * 1024 * 1024
 
 epsilon = 1e-05
@@ -44,8 +44,8 @@
 
 
 def eliminate_kernel(scale, part_rows, where_ref, scalar_ref, inverse_ref, inner_ref, cross_ref, weight_ref,
-                     mask_ref, product_ref, inputs_ref, panel_ref, whole_ref, pruned_ref, aux_ref, out_ref,
-                     state, dropped, errors, ring, own_product, sems):
+                     mask_ref, product_ref, inputs_ref, panel_ref, pruned_ref, aux_ref, out_ref,
+                     state, dropped, errors):
     count = 2 * BLOCK
     depth = count * 8
     sheets = state.shape[0] // depth
@@ -59,27 +59,6 @@
     def plane(q, j):
         return slice(q * depth + j * 8, q * depth + (j + 1) * 8)
 
-    tile_index = pl.program_id(0)
-    slots, chunk, _ = ring.shape
-
-    def fetch(tile, slot):
-        row = pl.multiple_of(tile * part_rows + part_rows // 2 + slot * chunk, chunk)
-        return chunk_copy(whole_ref, ring.at[slot], sems.at[slot], row)
-
-    @pl.when(tile_index == 0)
-    def _():
-        for slot in range(slots):
-            fetch(0, slot).start()
-
-    def multiply(slot):
-        fetch(tile_index, slot).wait()
-        own_product[:, slot * chunk : (slot + 1) * chunk] = nt_dot(inputs_ref[:, count:], ring[slot])
-
-    def renew(slot):
-        @pl.when(tile_index + 1 < pl.num_programs(0))
-        def _():
-            fetch(tile_index + 1, slot).start()
-
     eye = identity(count)
     columns = nt_dot(eye, weight_ref[...])
     drops = nt_dot(eye, (1 - mask_ref[...]).astype(jnp.float32).astype(jnp.bfloat16))
@@ -99,10 +78,6 @@
     for block in range(2):
         for part in range(BLOCK // SUB):
             first = block * BLOCK + part * SUB
-            spread = 2 * (BLOCK // SUB) // slots
-            slot, at_slot = divmod(block * (BLOCK // SUB) + part, spread)
-            if at_slot == spread // 2:
-                multiply(slot)
             planes = [[state[plane(q, first + i), :] for q in range(sheets)] for i in range(SUB)]
             for i in range(SUB):
                 j = first + i
@@ -122,8 +97,6 @@
             if left:
                 factor = inner_ref[block * (BLOCK // SUB) + part, after : after + left, :]
                 subtract(nn_dot(factor, stacked(first, SUB)), after, left)
-            if at_slot == spread - 1:
-                renew(slot)
         if block == 0:
             subtract(nn_dot(cross_ref[...], stacked(0, BLOCK)), BLOCK, BLOCK)
 
@@ -134,14 +107,12 @@
         aux_ref[count:, where] = errors[place(g, q, 0, count), :].astype(jnp.bfloat16)
         pruned_ref[where, :] = nt_dot(small, kept).astype(jnp.bfloat16)
 
-    half = part_rows // 2
-    step = min(512, half)
+    step = min(512, part_rows)
     for first in range(0, part_rows, step):
         place = slice(first, first + step)
         change = corrected(inputs_ref[:, :count], panel_ref[...], aux_ref, place)
-        source, at = (product_ref, first) if first < half else (own_product, first - half)
-        value = source[:, at : at + step] + change
-        base = tile_index * part_rows + first
+        value = product_ref[:, place] + change
+        base = pl.program_id(0) * part_rows + first
         out_ref[:, place] = units_of(value, inputs_ref, where_ref, base, scale)
 
 
@@ -152,7 +123,6 @@
 def eliminate(weight, factor, mask, where, product, inputs, panel_inputs, scale):
     count = 2 * BLOCK
     given = weight.shape[0]
-    whole = weight
     rows = pl.cdiv(given, 1024) * 1024
     if rows != given:
         more = ((0, rows - given), (0, 0))
@@ -172,8 +142,6 @@
     smem = pl.BlockSpec(memory_space=pltpu.SMEM)
     tokens = inputs.shape[0]
     part = min(given, tile)
-    chunk = min(256, part // 2)
-    slots = part // 2 // chunk
     hbm = pltpu.MemorySpace.HBM
     pruned, aux, units = pl.pallas_call(
         functools.partial(eliminate_kernel, scale, part),
@@ -186,10 +154,9 @@
             pl.BlockSpec((BLOCK, count), lambda i: (0, 0)),
             pl.BlockSpec((tile, count), lambda i: (i, 0)),
             pl.BlockSpec((tile, count), lambda i: (i, 0)),
-            pl.BlockSpec((tokens, part // 2), lambda i: (0, i)),
+            pl.BlockSpec((tokens, part), lambda i: (0, i)),
             pl.BlockSpec(inputs.shape, lambda i: (0, 0)),
             pl.BlockSpec((tokens, count), lambda i: (0, 0)),
-            pl.BlockSpec(memory_space=hbm),
         ],
         out_specs=[
             pl.BlockSpec((tile, count), lambda i: (i, 0)),
@@ -201,11 +168,7 @@
             hbm((2 * count, rows), jnp.bfloat16),
             jax.ShapeDtypeStruct((tokens, given), jnp.bfloat16),
         ],
-        scratch_shapes=[pltpu.VMEM((tile * count // 128, 128), jnp.float32)] * 3 + [
-            pltpu.VMEM((slots, chunk, inputs.shape[1] - count), jnp.bfloat16),
-            pltpu.VMEM((tokens, part // 2), jnp.float32),
-            pltpu.SemaphoreType.DMA((slots,)),
-        ],
+        scratch_shapes=[pltpu.VMEM((tile * count // 128, 128), jnp.float32)] * 3,
         compiler_params=pltpu.CompilerParams(vmem_limit_bytes=ELIMINATE_VMEM),
         cost_estimate=pl.CostEstimate(
             flops=2 * rows * count * count, bytes_accessed=rows * count * 12, transcendentals=0
@@ -213,7 +176,7 @@
         name="eliminate",
     )(
         where, scalars, inverse, inner, cross, weight,
-        pltpu.with_memory_space_constraint(mask, hbm), product, inputs, panel_inputs, whole,
+        pltpu.with_memory_space_constraint(mask, hbm), product, inputs, panel_inputs,
     )
     return pruned[:given], aux[:, :given], units
 
@@ -302,20 +265,19 @@
     return begin, run
 
 
-def first_kernel(part_rows, inputs_ref, weight_ref, product_ref, ring, ring_sems):
+def first_kernel(inputs_ref, weight_ref, product_ref, ring, ring_sems):
     chunk, width = ring.shape[1:]
     skipped = weight_ref.shape[1] - width
-    each = part_rows // 2 // chunk
-
-    def row_of(index):
-        return pl.multiple_of(index // each * part_rows + index % each * chunk, chunk)
+
+    def place_of(index):
+        return pl.multiple_of(index * chunk, chunk)
 
     def use(index, product):
-        product_ref[:, pl.ds(pl.multiple_of(index * chunk, chunk), chunk)] = product
+        product_ref[:, pl.ds(place_of(index), chunk)] = product
 
     total = product_ref.shape[1] // chunk
     begin, run = stream(
-        weight_ref, ring, ring_sems, total, row_of, lambda: inputs_ref[:, skipped:], use
+        weight_ref, ring, ring_sems, total, place_of, lambda: inputs_ref[:, skipped:], use
     )
     begin()
     run()
@@ -325,21 +287,20 @@
     tokens, features = inputs.shape
     rows = weight.shape[0]
     width = features - 2 * BLOCK
-    part = min(rows, tile_rows(rows))
-    chunk = min(256, part // 2)
-    ring = (min(6, rows // 2 // chunk), chunk, width)
+    chunk = min(256, rows // 2)
+    ring = (min(6, rows // chunk), chunk, width)
     return pl.pallas_call(
-        functools.partial(first_kernel, part),
+        first_kernel,
         in_specs=[
             pl.BlockSpec(memory_space=pltpu.VMEM),
             pl.BlockSpec(memory_space=pltpu.MemorySpace.HBM),
         ],
         out_specs=pl.BlockSpec(memory_space=pltpu.VMEM),
-        out_shape=jax.ShapeDtypeStruct((tokens, rows // 2), jnp.float32),
+        out_shape=jax.ShapeDtypeStruct((tokens, rows), jnp.float32),
         scratch_shapes=[pltpu.VMEM(ring, jnp.bfloat16), pltpu.SemaphoreType.DMA((ring[0],))],
         compiler_params=pltpu.CompilerParams(vmem_limit_bytes=32 * 1024 * 1024),
         cost_estimate=pl.CostEstimate(
-            flops=tokens * rows * width, bytes_accessed=rows * width, transcendentals=0
+            flops=2 * tokens * rows * width, bytes_accessed=rows * width * 2, transcendentals=0
         ),
         name="first_product",
     )(inputs, weight)
@@ -406,7 +367,10 @@
             flops=2 * tokens * rows * features, bytes_accessed=rows * width * 2, transcendentals=0
         ),
         name="turn_product",
-    )(where, inputs, weight, panel, aux)
+    )(
+        where, inputs, weight,
+        *(pltpu.with_memory_space_constraint(a, pltpu.MemorySpace.HBM) for a in (panel, aux)),
+    )
 
 
 def per_device(tokens, up_weight, hess_panel, keep_mask):

time: 269 us -> 273 us (1.015)
  Pallas kernels: 116 us -> 136 us
  local copies, waits for them, and re-layouts: 17.8 us -> 4.67 us
    pallas_call x3, Pallas kernels: 70.9 us -> 91.6 us  [turn_product(): pl.pallas_call(functools.partial(turn_kernel, scale), in_specs=[pl.BlockS...]
    unnamed x15 -> x3, local copies, waits for them, and re-layouts: 13.2 us -> 0.11 us
    pallas_call x1, Pallas kernels: 31.5 us -> 20.5 us  [eliminate(): pl.pallas_call(functools.partial(eliminate_kernel, scale, part), grid=(ro...]
    pallas_call x1, Pallas kernels: 12.4 us -> 22 us  [first_product(): pl.pallas_call(first_kernel, in_specs=[pl.BlockSpec(memory_space=pltpu.VM...]
  transfers between devices with their start and end apart: 3 -> 3, of which waited for: 2 -> 1; matrix products, arithmetic and copies ran while one was open for 2% -> 2% of each run, Pallas kernels for 16% -> 16%
where the time goes in v1:
time: 273 us; the launch traced here: 272 us
  Pallas kernels  136 us (50%)
  blocking collectives  99.1 us (36%)
  between operations  14.4 us (5%)
  starting transfers between devices  6.82 us (2%)
  waiting for transfers between devices  6.74 us (2%)
  local copies, waits for them, and re-layouts  4.67 us (2%)
  other arithmetic  3.58 us (1%)
    pallas_call x3, Pallas kernels, turn_product(): pl.pallas_call(functools.partial(turn_kernel, scale), in_specs=[pl.BlockS...  91.6 us
    all_to_all x3, blocking collectives, per_device(): lax.all_to_all(jnp.concatenate([units, units], 0), ('layer', 'row'), spli...  43.6 us
    all_to_all x3, blocking collectives, per_device(): copies = lax.all_to_all(copies, 'row', split_axis=0, concat_axis=0)  36.8 us
    pallas_call x1, Pallas kernels, first_product(): pl.pallas_call(first_kernel, in_specs=[pl.BlockSpec(memory_space=pltpu.VM...  22 us
    pallas_call x1, Pallas kernels, eliminate(): pl.pallas_call(functools.partial(eliminate_kernel, scale, part), grid=(ro...  20.5 us
    all_to_all x1, blocking collectives, per_device(): lax.all_to_all(jnp.concatenate([token_share, factor_share], 1), 'row', sp...  18.7 us
    all_to_all x1, waiting for transfers between devices, per_device(): spread = lax.all_to_all(units, 'row', split_axis=0, concat_axis=0)  6.7 us
  transfers between devices with their start and end apart: 3, of which 1 were waited for; matrix products, arithmetic and copies ran while one was open for 2% of the time, Pallas kernels for 16%

profile of v1, /device:TPU:0, one launch (start us, length us, event | category | flops | bytes accessed | tf_op | source)
XLA Modules:
  0.0 272.2 jit_solution(9651731109368896917)
XLA Ops:
  7.2 0.0 all-gather.2.cloned.1.call-start
  7.2 1.3 convert_bitcast_fusion
  8.5 0.8 broadcast_in_dim.32
  9.4 18.7 %all_to_all.45 = bf16[8,96,256]{2,1,0:T(8,128)(2,1)S(1)} all-to-all(bf16[8,96,256]{2,1,0:T(8,128)(2,1)S(1)} %pad_maximum_fusion), channel_id=1, replica_groups=mesh['layer'=4,'row'=8] {'row'}, dimensions={0} | all-to-all | bytes 786432 | tf_op jit(solution)/shard_map/all_to_all | solution.py:394
  28.1 0.0 all-gather.2.cloned.1.call-update
  28.2 0.1 reshape.102.inputs_ref
  28.4 1.3 subtract_convert_fusion
  29.7 0.7 broadcast_in_dim.35
  30.4 3.4 %all-to-all-start.1 = ((bf16[8,64,256]{2,1,0:T(8,128)(2,1)}), bf16[8,64,256]{2,1,0:T(8,128)(2,1)S(1)}, u32[]{:S(2)}, u32[]{:S(2)}) async-start(bf16[8,64,256]{2,1,0:T(8,128)(2,1)} %broadcast_in_dim.35), calls=%async_computation.1 | async-start | bytes 524288 | tf_op jit(solution)/shard_map/all_to_all | solution.py:21
  33.8 0.1 pad_add_fusion.where_ref
  33.9 22.0 %first_product.1.product_ref = f32[16,4096]{1,0:T(8,128)S(1)} custom-call(bf16[16,8192]{1,0:T(8,128)(2,1)S(1)} %reshape.102.inputs_ref, bf16[4096,8192]{1,0:T(8,128)(2,1)} %bitcast.10.weight_ref), custom_call_target="tpu_custom_call" | custom-call | flops 1040187392 | bytes 65011712 | tf_op jit(solution)/shard_map/first_product/pallas_call | solution.py:292
  55.9 0.4 copy.15
  56.4 0.3 reshape.114
  56.7 0.2 select_reduce_fusion.1
  56.9 0.1 copy.16
  57.0 0.1 reshape.103.scalar_ref
  57.1 0.5 copy.18.inner_ref
  57.6 0.1 copy.19
  57.7 0.2 convert_reduce_fusion
  57.9 0.1 div.30.inverse_ref
  58.0 20.5 %eliminate.1 = (bf16[4096,256]{1,0:T(8,128)(2,1)}, bf16[512,4096]{1,0:T(8,128)(2,1)}, bf16[16,4096]{1,0:T(8,128)(2,1)S(1)}) custom-call(s32[2]{0:T(128)S(1)} %pad_add_fusion.where_ref, f32[4096]{0:T(1024)S(1)} %reshape.103.scalar_ref, f32[256]{0:T(256)S(1)} %div.30.inverse_ref, bf16[16,256,32]{2,1,0:T(8,128)(2,1)S(1)} %copy.18.inner_ref, ...), custom_call_target="tpu_custom_call" | custom-call | flops 536870912 | bytes 12582912 | tf_op jit(solution)/shard_map/eliminate/pallas_call | solution.py:146
  78.6 0.1 reshape.106
  78.7 0.3 pad_maximum_fusion.2
  79.0 15.9 %all_to_all.46.spread_ref = bf16[16,2,4096]{2,1,0:T(2,128)(2,1)S(1)} all-to-all(bf16[16,2,4096]{2,1,0:T(2,128)(2,1)S(1)} %pad_maximum_fusion.2), channel_id=1, replica_groups={{0,1,2,3,4,5,6,7,8,9,10,11,12,13,14,15},{16,17,18,19,20,21,22,23,24,25,..., dimensions={0} | all-to-all | bytes 524288 | tf_op jit(solution)/shard_map/all_to_all | solution.py:434
  94.9 0.2 fold.4
  95.1 12.3 %all_to_all.47 = bf16[8,2,8192]{2,1,0:T(2,128)(2,1)S(1)} all-to-all(bf16[8,2,8192]{2,1,0:T(2,128)(2,1)S(1)} %get-tuple-element.21), channel_id=1, replica_groups=mesh['layer'=4,'row'=8] {'row'}, dimensions={0} | all-to-all | bytes 524288 | tf_op jit(solution)/shard_map/all_to_all | solution.py:440
  107.4 0.1 reshape.107.inputs_ref
  107.6 0.0 all-gather.2.cloned.1.call-done.panel_ref
  107.6 30.5 %turn_product.3 = bf16[16,4096]{1,0:T(8,128)(2,1)S(1)} custom-call(s32[2]{0:T(128)S(1)} %pad_add_fusion.where_ref, bf16[16,8192]{1,0:T(8,128)(2,1)S(1)} %reshape.107.inputs_ref, bf16[4096,8192]{1,0:T(8,128)(2,1)} %bitcast.10.weight_ref, bf16[256,8192]{1,0:T(8,128)(2,1)} %all-gather.2.cloned.1.call-done.panel_ref, bf16[512,4096]{1,0:T(8,128)(2,1)} %get-tuple-element.22.aux_ref), custom_call_target="tpu_custom_call" | custom-call | flops 1073741824 | bytes 65011712 | tf_op jit(solution)/shard_map/turn_product/pallas_call | solution.py:352
  138.1 0.1 reshape.108
  138.2 0.3 pad_maximum_fusion.3
  138.6 14.3 %all_to_all.48.spread_ref = bf16[16,2,4096]{2,1,0:T(2,128)(2,1)S(1)} all-to-all(bf16[16,2,4096]{2,1,0:T(2,128)(2,1)S(1)} %pad_maximum_fusion.3), channel_id=1, replica_groups={{8,9,10,11,12,13,14,15,16,17,18,19,20,21,22,23},{0,1,2,3,4,5,6,7,24,25,..., dimensions={0} | all-to-all | bytes 524288 | tf_op jit(solution)/shard_map/all_to_all | solution.py:434
  152.9 0.2 fold.5
  153.1 12.2 %all_to_all.49 = bf16[8,2,8192]{2,1,0:T(2,128)(2,1)S(1)} all-to-all(bf16[8,2,8192]{2,1,0:T(2,128)(2,1)S(1)} %get-tuple-element.23), channel_id=1, replica_groups=mesh['layer'=4,'row'=8] {'row'}, dimensions={0} | all-to-all | bytes 524288 | tf_op jit(solution)/shard_map/all_to_all | solution.py:440
  165.3 0.1 reshape.109.inputs_ref
  165.4 30.5 %turn_product.4 = bf16[16,4096]{1,0:T(8,128)(2,1)S(1)} custom-call(s32[2]{0:T(128)S(1)} %pad_add_fusion.where_ref, bf16[16,8192]{1,0:T(8,128)(2,1)S(1)} %reshape.109.inputs_ref, bf16[4096,8192]{1,0:T(8,128)(2,1)} %bitcast.10.weight_ref, bf16[256,8192]{1,0:T(8,128)(2,1)} %all-gather.2.cloned.1.call-done.panel_ref, bf16[512,4096]{1,0:T(8,128)(2,1)} %get-tuple-element.22.aux_ref), custom_call_target="tpu_custom_call" | custom-call | flops 1073741824 | bytes 65011712 | tf_op jit(solution)/shard_map/turn_product/pallas_call | solution.py:352
  196.0 0.1 reshape.110
  196.1 0.3 pad_maximum_fusion.4
  196.4 13.4 %all_to_all.50.spread_ref = bf16[16,2,4096]{2,1,0:T(2,128)(2,1)S(1)} all-to-all(bf16[16,2,4096]{2,1,0:T(2,128)(2,1)S(1)} %pad_maximum_fusion.4), channel_id=1, replica_groups={{16,17,18,19,20,21,22,23,24,25,26,27,28,29,30,31},{0,1,2,3,4,5,6,7,8,9,..., dimensions={0} | all-to-all | bytes 524288 | tf_op jit(solution)/shard_map/all_to_all | solution.py:434
  209.8 0.2 fold.6
  210.0 12.2 %all_to_all.51 = bf16[8,2,8192]{2,1,0:T(2,128)(2,1)S(1)} all-to-all(bf16[8,2,8192]{2,1,0:T(2,128)(2,1)S(1)} %get-tuple-element.24), channel_id=1, replica_groups=mesh['layer'=4,'row'=8] {'row'}, dimensions={0} | all-to-all | bytes 524288 | tf_op jit(solution)/shard_map/all_to_all | solution.py:440
  222.3 0.1 reshape.111.inputs_ref
  222.4 30.5 %turn_product.5 = bf16[16,4096]{1,0:T(8,128)(2,1)S(1)} custom-call(s32[2]{0:T(128)S(1)} %pad_add_fusion.where_ref, bf16[16,8192]{1,0:T(8,128)(2,1)S(1)} %reshape.111.inputs_ref, bf16[4096,8192]{1,0:T(8,128)(2,1)} %bitcast.10.weight_ref, bf16[256,8192]{1,0:T(8,128)(2,1)} %all-gather.2.cloned.1.call-done.panel_ref, bf16[512,4096]{1,0:T(8,128)(2,1)} %get-tuple-element.22.aux_ref), custom_call_target="tpu_custom_call" | custom-call | flops 1073741824 | bytes 65011712 | tf_op jit(solution)/shard_map/turn_product/pallas_call | solution.py:352
  252.9 0.8 reshape.112
  253.7 3.4 %all-to-all-start.8 = ((bf16[8,2,4096]{2,1,0:T(2,128)(2,1)}), bf16[8,2,4096]{2,1,0:T(2,128)(2,1)S(1)}, u32[]{:S(2)}, u32[]{:S(2)}) async-start(bf16[8,2,4096]{2,1,0:T(2,128)(2,1)} %reshape.112), calls=%async_computation.8 | async-start | bytes 262144 | tf_op jit(solution)/shard_map/all_to_all | solution.py:426
  257.1 6.7 %all-to-all-done.8.spread_ref = bf16[8,2,4096]{2,1,0:T(2,128)(2,1)S(1)} async-done(((bf16[8,2,4096]{2,1,0:T(2,128)(2,1)}), bf16[8,2,4096]{2,1,0:T(2,128)(2,1)S(1)}, u32[]{:S(2)}, u32[]{:S(2)}) %all-to-all-start.8) | async-done | bytes 131104 | tf_op jit(solution)/shard_map/all_to_all | solution.py:426
  263.8 0.9 fold.7
  264.7 0.7 fusion.4
  (21 shorter events, 0.2 us)
Async XLA Ops:
  7.2 100.4 %all-gather.2.cloned.1.call-start = ((), (), s32[]{:S(2)}) async-start(), calls=%async_computation.9 | async-start | bytes 4718592 | tf_op jit(solution)/shard_map/all_gather | solution.py:399
  8.5 19.6 %copy-start = (bf16[256,1024]{1,0:T(8,128)(2,1)}, bf16[256,1024]{1,0:T(8,128)(2,1)S(1)}, u32[]{:S(2)}) copy-start(bf16[256,1024]{1,0:T(8,128)(2,1)S(1)} %convert_bitcast_fusion) | copy-start | bytes 1572868
  30.4 25.5 %all-to-all-start.1 = ((bf16[8,64,256]{2,1,0:T(8,128)(2,1)}), bf16[8,64,256]{2,1,0:T(8,128)(2,1)S(1)}, u32[]{:S(2)}, u32[]{:S(2)}) async-start(bf16[8,64,256]{2,1,0:T(8,128)(2,1)} %broadcast_in_dim.35), calls=%async_computation.1 | async-start | bytes 524288 | tf_op jit(solution)/shard_map/all_to_all | solution.py:21
  253.7 10.1 %all-to-all-start.8 = ((bf16[8,2,4096]{2,1,0:T(2,128)(2,1)}), bf16[8,2,4096]{2,1,0:T(2,128)(2,1)S(1)}, u32[]{:S(2)}, u32[]{:S(2)}) async-start(bf16[8,2,4096]{2,1,0:T(2,128)(2,1)} %reshape.112), calls=%async_computation.8 | async-start | bytes 262144 | tf_op jit(solution)/shard_map/all_to_all | solution.py:426
Sparse Core Ops, SparseCore 0:
  28.2 50.8 all-gather.1

commit v2 on v1

--- a/solution.py
+++ b/solution.py
@@ -238,29 +238,33 @@
     )
 
 
-def stream(weight_ref, ring, ring_sems, total, row_of, inputs, use):
+def stream(weight_ref, ring, ring_sems, total, row_of, inputs):
     slots = ring.shape[0]
 
     def copy(index, slot):
         return chunk_copy(weight_ref, ring.at[slot], ring_sems.at[slot], row_of(index))
 
+    ahead = slots - 1
+
     def begin():
-        for index in range(slots):
+        for index in range(ahead):
             copy(index, index).start()
 
-    def step(index, _):
-        slot = lax.rem(index, slots)
-        copy(index, slot).wait()
-        use(index, nt_dot(inputs(), ring[slot]))
-
-        @pl.when(index + slots < total)
-        def _():
-            copy(index + slots, slot).start()
-
-        return 0
-
-    def run():
-        lax.fori_loop(0, total, step, 0)
+    def run(first, last, use, besides=None):
+        def step(index, _):
+            slot = lax.rem(index, slots)
+            copy(index, slot).wait()
+
+            @pl.when(index + ahead < total)
+            def _():
+                copy(index + ahead, lax.rem(index + ahead, slots)).start()
+
+            if besides is not None:
+                pl.when(index == first)(besides)
+            use(index, nt_dot(inputs(), ring[slot]))
+            return 0
+
+        lax.fori_loop(first, last, step, 0)
 
     return begin, run
 
@@ -277,10 +281,10 @@
 
     total = product_ref.shape[1] // chunk
     begin, run = stream(
-        weight_ref, ring, ring_sems, total, place_of, lambda: inputs_ref[:, skipped:], use
+        weight_ref, ring, ring_sems, total, place_of, lambda: inputs_ref[:, skipped:]
     )
     begin()
-    run()
+    run(0, total, use)
 
 
 def first_product(inputs, weight):
@@ -288,7 +292,7 @@
     rows = weight.shape[0]
     width = features - 2 * BLOCK
     chunk = min(256, rows // 2)
-    ring = (min(6, rows // chunk), chunk, width)
+    ring = (min(4, rows // chunk), chunk, width)
     return pl.pallas_call(
         first_kernel,
         in_specs=[
@@ -319,25 +323,39 @@
         value = product + change[:, place]
         out_ref[:, place] = units_of(value, inputs_ref, where_ref, place_of(index), scale)
 
+    def keep(index, product):
+        change[:, pl.ds(place_of(index), chunk)] = product
+
     rows = change.shape[1]
+    total = rows // chunk
+    early = total // 2
     begin, run = stream(
-        weight_ref, ring, ring_sems, rows // chunk, place_of, lambda: inputs_ref[:, skipped:], use
+        weight_ref, ring, ring_sems, total, place_of, lambda: inputs_ref[:, skipped:]
     )
     panel_copy = pltpu.make_async_copy(
         panel_ref.at[:, pl.ds(skipped, width)], panel, side_sems.at[0]
     )
     aux_copy = pltpu.make_async_copy(aux_ref, aux, side_sems.at[1])
-    panel_copy.start()
-    aux_copy.start()
+
+    def start_sides():
+        panel_copy.start()
+        aux_copy.start()
+
     begin()
+    run(0, early, keep, start_sides)
     panel_copy.wait()
     panel_inputs = nt_dot(inputs_ref[:, skipped:], panel[...])
     aux_copy.wait()
-    step = min(1024, rows)
+    step = min(1024, early * chunk)
     for first in range(0, rows, step):
         place = slice(first, first + step)
-        change[:, place] = corrected(inputs_ref[:, :skipped], panel_inputs, aux, place)
-    run()
+        part = corrected(inputs_ref[:, :skipped], panel_inputs, aux, place)
+        if first < early * chunk:
+            value = change[:, place] + part
+            out_ref[:, place] = units_of(value, inputs_ref, where_ref, first, scale)
+        else:
+            change[:, place] = part
+    run(early, total, use)
 
 
 def turn_product(where, inputs, weight, panel, aux, scale):
@@ -346,7 +364,7 @@
     count = 2 * BLOCK
     width = features - count
     chunk = min(256, rows // 2)
-    ring = (min(6, rows // chunk), chunk, width)
+    ring = (min(4, rows // chunk), chunk, width)
     vmem = pl.BlockSpec(memory_space=pltpu.VMEM)
     hbm = pl.BlockSpec(memory_space=pltpu.MemorySpace.HBM)
     return pl.pallas_call(

time: 273 us -> 264 us (0.967)
  Pallas kernels: 136 us -> 127 us
    pallas_call x3, Pallas kernels: 91.6 us -> 82.6 us  [turn_product(): pl.pallas_call(functools.partial(turn_kernel, scale), in_specs=[pl.BlockS...]
where the time goes in v2:
time: 264 us; the launch traced here: 263 us
  Pallas kernels  127 us (48%)
  blocking collectives  99.1 us (38%)
  between operations  14.4 us (5%)
  starting transfers between devices  6.82 us (3%)
  waiting for transfers between devices  6.74 us (3%)
  local copies, waits for them, and re-layouts  4.67 us (2%)
  other arithmetic  3.58 us (1%)
    pallas_call x3, Pallas kernels, turn_product(): pl.pallas_call(functools.partial(turn_kernel, scale), in_specs=[pl.BlockS...  82.6 us
    all_to_all x3, blocking collectives, per_device(): lax.all_to_all(jnp.concatenate([units, units], 0), ('layer', 'row'), spli...  43.6 us
    all_to_all x3, blocking collectives, per_device(): copies = lax.all_to_all(copies, 'row', split_axis=0, concat_axis=0)  36.8 us
    pallas_call x1, Pallas kernels, first_product(): pl.pallas_call(first_kernel, in_specs=[pl.BlockSpec(memory_space=pltpu.VM...  22 us
    pallas_call x1, Pallas kernels, eliminate(): pl.pallas_call(functools.partial(eliminate_kernel, scale, part), grid=(ro...  20.5 us
    all_to_all x1, blocking collectives, per_device(): lax.all_to_all(jnp.concatenate([token_share, factor_share], 1), 'row', sp...  18.7 us
    all_to_all x1, waiting for transfers between devices, per_device(): spread = lax.all_to_all(units, 'row', split_axis=0, concat_axis=0)  6.7 us
  transfers between devices with their start and end apart: 3, of which 1 were waited for; matrix products, arithmetic and copies ran while one was open for 2% of the time, Pallas kernels for 16%

profile of v2, /device:TPU:0, one launch (start us, length us, event | category | flops | bytes accessed | tf_op | source)
XLA Modules:
  0.0 263.3 jit_solution(1034886312614636454)
XLA Ops:
  7.2 0.0 all-gather.2.cloned.1.call-start
  7.2 1.3 convert_bitcast_fusion
  8.5 0.8 broadcast_in_dim.32
  9.4 18.7 %all_to_all.45 = bf16[8,96,256]{2,1,0:T(8,128)(2,1)S(1)} all-to-all(bf16[8,96,256]{2,1,0:T(8,128)(2,1)S(1)} %pad_maximum_fusion), channel_id=1, replica_groups=mesh['layer'=4,'row'=8] {'row'}, dimensions={0} | all-to-all | bytes 786432 | tf_op jit(solution)/shard_map/all_to_all | solution.py:412
  28.1 0.0 all-gather.2.cloned.1.call-update
  28.2 0.1 reshape.102.inputs_ref
  28.4 1.3 subtract_convert_fusion
  29.7 0.7 broadcast_in_dim.35
  30.4 3.4 %all-to-all-start.1 = ((bf16[8,64,256]{2,1,0:T(8,128)(2,1)}), bf16[8,64,256]{2,1,0:T(8,128)(2,1)S(1)}, u32[]{:S(2)}, u32[]{:S(2)}) async-start(bf16[8,64,256]{2,1,0:T(8,128)(2,1)} %broadcast_in_dim.35), calls=%async_computation.1 | async-start | bytes 524288 | tf_op jit(solution)/shard_map/all_to_all | solution.py:21
  33.8 0.1 pad_add_fusion.where_ref
  33.9 22.0 %first_product.1.product_ref = f32[16,4096]{1,0:T(8,128)S(1)} custom-call(bf16[16,8192]{1,0:T(8,128)(2,1)S(1)} %reshape.102.inputs_ref, bf16[4096,8192]{1,0:T(8,128)(2,1)} %bitcast.10.weight_ref), custom_call_target="tpu_custom_call" | custom-call | flops 1040187392 | bytes 65011712 | tf_op jit(solution)/shard_map/first_product/pallas_call | solution.py:296
  56.0 0.4 copy.15
  56.4 0.3 reshape.114
  56.7 0.2 select_reduce_fusion.1
  56.9 0.1 copy.16
  57.0 0.1 reshape.103.scalar_ref
  57.2 0.5 copy.18.inner_ref
  57.7 0.1 copy.19
  57.8 0.2 convert_reduce_fusion
  58.0 0.1 div.30.inverse_ref
  58.1 20.5 %eliminate.1 = (bf16[4096,256]{1,0:T(8,128)(2,1)}, bf16[512,4096]{1,0:T(8,128)(2,1)}, bf16[16,4096]{1,0:T(8,128)(2,1)S(1)}) custom-call(s32[2]{0:T(128)S(1)} %pad_add_fusion.where_ref, f32[4096]{0:T(1024)S(1)} %reshape.103.scalar_ref, f32[256]{0:T(256)S(1)} %div.30.inverse_ref, bf16[16,256,32]{2,1,0:T(8,128)(2,1)S(1)} %copy.18.inner_ref, ...), custom_call_target="tpu_custom_call" | custom-call | flops 536870912 | bytes 12582912 | tf_op jit(solution)/shard_map/eliminate/pallas_call | solution.py:146
  78.6 0.1 reshape.106
  78.7 0.3 pad_maximum_fusion.2
  79.1 15.9 %all_to_all.46.spread_ref = bf16[16,2,4096]{2,1,0:T(2,128)(2,1)S(1)} all-to-all(bf16[16,2,4096]{2,1,0:T(2,128)(2,1)S(1)} %pad_maximum_fusion.2), channel_id=1, replica_groups={{0,1,2,3,4,5,6,7,8,9,10,11,12,13,14,15},{16,17,18,19,20,21,22,23,24,25,..., dimensions={0} | all-to-all | bytes 524288 | tf_op jit(solution)/shard_map/all_to_all | solution.py:452
  95.0 0.2 fold.4
  95.2 12.3 %all_to_all.47 = bf16[8,2,8192]{2,1,0:T(2,128)(2,1)S(1)} all-to-all(bf16[8,2,8192]{2,1,0:T(2,128)(2,1)S(1)} %get-tuple-element.21), channel_id=1, replica_groups=mesh['layer'=4,'row'=8] {'row'}, dimensions={0} | all-to-all | bytes 524288 | tf_op jit(solution)/shard_map/all_to_all | solution.py:458
  107.5 0.1 reshape.107.inputs_ref
  107.6 0.0 all-gather.2.cloned.1.call-done.panel_ref
  107.6 27.5 %turn_product.3 = bf16[16,4096]{1,0:T(8,128)(2,1)S(1)} custom-call(s32[2]{0:T(128)S(1)} %pad_add_fusion.where_ref, bf16[16,8192]{1,0:T(8,128)(2,1)S(1)} %reshape.107.inputs_ref, bf16[4096,8192]{1,0:T(8,128)(2,1)} %bitcast.10.weight_ref, bf16[256,8192]{1,0:T(8,128)(2,1)} %all-gather.2.cloned.1.call-done.panel_ref, bf16[512,4096]{1,0:T(8,128)(2,1)} %get-tuple-element.22.aux_ref), custom_call_target="tpu_custom_call" | custom-call | flops 1073741824 | bytes 65011712 | tf_op jit(solution)/shard_map/turn_product/pallas_call | solution.py:370
  135.2 0.1 reshape.108
  135.3 0.3 pad_maximum_fusion.3
  135.7 14.3 %all_to_all.48.spread_ref = bf16[16,2,4096]{2,1,0:T(2,128)(2,1)S(1)} all-to-all(bf16[16,2,4096]{2,1,0:T(2,128)(2,1)S(1)} %pad_maximum_fusion.3), channel_id=1, replica_groups={{8,9,10,11,12,13,14,15,16,17,18,19,20,21,22,23},{0,1,2,3,4,5,6,7,24,25,..., dimensions={0} | all-to-all | bytes 524288 | tf_op jit(solution)/shard_map/all_to_all | solution.py:452
  150.0 0.2 fold.5
  150.2 12.2 %all_to_all.49 = bf16[8,2,8192]{2,1,0:T(2,128)(2,1)S(1)} all-to-all(bf16[8,2,8192]{2,1,0:T(2,128)(2,1)S(1)} %get-tuple-element.23), channel_id=1, replica_groups=mesh['layer'=4,'row'=8] {'row'}, dimensions={0} | all-to-all | bytes 524288 | tf_op jit(solution)/shard_map/all_to_all | solution.py:458
  162.4 0.1 reshape.109.inputs_ref
  162.5 27.5 %turn_product.4 = bf16[16,4096]{1,0:T(8,128)(2,1)S(1)} custom-call(s32[2]{0:T(128)S(1)} %pad_add_fusion.where_ref, bf16[16,8192]{1,0:T(8,128)(2,1)S(1)} %reshape.109.inputs_ref, bf16[4096,8192]{1,0:T(8,128)(2,1)} %bitcast.10.weight_ref, bf16[256,8192]{1,0:T(8,128)(2,1)} %all-gather.2.cloned.1.call-done.panel_ref, bf16[512,4096]{1,0:T(8,128)(2,1)} %get-tuple-element.22.aux_ref), custom_call_target="tpu_custom_call" | custom-call | flops 1073741824 | bytes 65011712 | tf_op jit(solution)/shard_map/turn_product/pallas_call | solution.py:370
  190.1 0.1 reshape.110
  190.2 0.3 pad_maximum_fusion.4
  190.6 13.4 %all_to_all.50.spread_ref = bf16[16,2,4096]{2,1,0:T(2,128)(2,1)S(1)} all-to-all(bf16[16,2,4096]{2,1,0:T(2,128)(2,1)S(1)} %pad_maximum_fusion.4), channel_id=1, replica_groups={{16,17,18,19,20,21,22,23,24,25,26,27,28,29,30,31},{0,1,2,3,4,5,6,7,8,9,..., dimensions={0} | all-to-all | bytes 524288 | tf_op jit(solution)/shard_map/all_to_all | solution.py:452
  203.9 0.2 fold.6
  204.2 12.2 %all_to_all.51 = bf16[8,2,8192]{2,1,0:T(2,128)(2,1)S(1)} all-to-all(bf16[8,2,8192]{2,1,0:T(2,128)(2,1)S(1)} %get-tuple-element.24), channel_id=1, replica_groups=mesh['layer'=4,'row'=8] {'row'}, dimensions={0} | all-to-all | bytes 524288 | tf_op jit(solution)/shard_map/all_to_all | solution.py:458
  216.4 0.1 reshape.111.inputs_ref
  216.5 27.5 %turn_product.5 = bf16[16,4096]{1,0:T(8,128)(2,1)S(1)} custom-call(s32[2]{0:T(128)S(1)} %pad_add_fusion.where_ref, bf16[16,8192]{1,0:T(8,128)(2,1)S(1)} %reshape.111.inputs_ref, bf16[4096,8192]{1,0:T(8,128)(2,1)} %bitcast.10.weight_ref, bf16[256,8192]{1,0:T(8,128)(2,1)} %all-gather.2.cloned.1.call-done.panel_ref, bf16[512,4096]{1,0:T(8,128)(2,1)} %get-tuple-element.22.aux_ref), custom_call_target="tpu_custom_call" | custom-call | flops 1073741824 | bytes 65011712 | tf_op jit(solution)/shard_map/turn_product/pallas_call | solution.py:370
  244.1 0.8 reshape.112
  244.8 3.4 %all-to-all-start.8 = ((bf16[8,2,4096]{2,1,0:T(2,128)(2,1)}), bf16[8,2,4096]{2,1,0:T(2,128)(2,1)S(1)}, u32[]{:S(2)}, u32[]{:S(2)}) async-start(bf16[8,2,4096]{2,1,0:T(2,128)(2,1)} %reshape.112), calls=%async_computation.8 | async-start | bytes 262144 | tf_op jit(solution)/shard_map/all_to_all | solution.py:444
  248.2 6.7 %all-to-all-done.8.spread_ref = bf16[8,2,4096]{2,1,0:T(2,128)(2,1)S(1)} async-done(((bf16[8,2,4096]{2,1,0:T(2,128)(2,1)}), bf16[8,2,4096]{2,1,0:T(2,128)(2,1)S(1)}, u32[]{:S(2)}, u32[]{:S(2)}) %all-to-all-start.8) | async-done | bytes 131104 | tf_op jit(solution)/shard_map/all_to_all | solution.py:444
  254.9 0.9 fold.7
  255.8 0.7 fusion.4
  (21 shorter events, 0.2 us)
Async XLA Ops:
  7.2 100.5 %all-gather.2.cloned.1.call-start = ((), (), s32[]{:S(2)}) async-start(), calls=%async_computation.9 | async-start | bytes 4718592 | tf_op jit(solution)/shard_map/all_gather | solution.py:417
  8.5 19.6 %copy-start = (bf16[256,1024]{1,0:T(8,128)(2,1)}, bf16[256,1024]{1,0:T(8,128)(2,1)S(1)}, u32[]{:S(2)}) copy-start(bf16[256,1024]{1,0:T(8,128)(2,1)S(1)} %convert_bitcast_fusion) | copy-start | bytes 1572868
  30.4 25.6 %all-to-all-start.1 = ((bf16[8,64,256]{2,1,0:T(8,128)(2,1)}), bf16[8,64,256]{2,1,0:T(8,128)(2,1)S(1)}, u32[]{:S(2)}, u32[]{:S(2)}) async-start(bf16[8,64,256]{2,1,0:T(8,128)(2,1)} %broadcast_in_dim.35), calls=%async_computation.1 | async-start | bytes 524288 | tf_op jit(solution)/shard_map/all_to_all | solution.py:21
  244.8 10.1 %all-to-all-start.8 = ((bf16[8,2,4096]{2,1,0:T(2,128)(2,1)}), bf16[8,2,4096]{2,1,0:T(2,128)(2,1)S(1)}, u32[]{:S(2)}, u32[]{:S(2)}) async-start(bf16[8,2,4096]{2,1,0:T(2,128)(2,1)} %reshape.112), calls=%async_computation.8 | async-start | bytes 262144 | tf_op jit(solution)/shard_map/all_to_all | solution.py:444
Sparse Core Ops, SparseCore 0:
  28.2 50.8 all-gather.1
